TPU v7x, 32 devices: a whole 2x2x4 slice. The times are simulated.
32 devices in a mesh: scen: 2 (over x), bus: 16 (over z, y, core).
Axes of the slice: x: 2, y: 2, z: 4, core: 2. Of those that a mesh axis runs over, the one named last changes fastest.
Arguments:
- injections: bfloat16 [256, 4096], P(('scen', 'bus')), may hold values from -6 to 6
- tile_values: bfloat16 [1024, 128, 128], P('bus', 'scen'), may hold values from -0.109375 to 0.109375
- tile_line: int32 [1024], P('bus'), may hold values from 0 to 47, as said below
- tile_bus: int32 [1024], P('bus'), may hold values from 0 to 1
- flow_pred: bfloat16 [256, 6144], P('scen', 'bus'), may hold values from -6 to 6
- line_limit: int32 [6144], P('bus'), may hold values from 50 to 199
Outputs:
- grad_injections: bfloat16 [256, 4096], P(('scen', 'bus'))
- flows: float32 [256, 6144], P('scen', 'bus')
Inputs may be any that keep to these rules, and one draw needn't show every extreme that they name: `tile_line`: tile t is held by bus index t // 64; line block b is owned by bus index b // 3. Of the 64 tiles of one bus index at most 6 have line blocks of one owner, and in every draw some owner gets exactly 6 tiles from every bus index. A pair of line block and bus block may occur in several tiles; their values add.
All inputs are finite; a program needn't handle non-finite values.
Results may differ from a plain program's by a relative error of at most 0.0039.
Values may be sent and summed in bfloat16 or wider, within the bound.
A program may use at most 64 MiB of HBM per device.

v0:
```python
import jax
import jax.numpy as jnp
from jax import lax
from jax.sharding import PartitionSpec as P


def per_device(injections, tile_values, tile_line, tile_bus, flow_pred, line_limit):
    bus_count = lax.axis_size("bus")
    local_inj = lax.all_to_all(injections, "bus", split_axis=1, concat_axis=0, tiled=True)
    tile_full = lax.all_gather(tile_values, "scen", axis=1, tiled=True)
    tile_count = tile_full.shape[0]
    tile_size = tile_full.shape[1]
    row_count = local_inj.shape[0]
    blocks_here = local_inj.shape[1] // tile_size
    line_blocks = flow_pred.shape[1] // tile_size
    per_owner = tile_count // bus_count
    capacity = per_owner + max(1, tile_count // (2 * bus_count))
    slot_total = bus_count * capacity
    inj_blocks = local_inj.reshape(row_count, blocks_here, tile_size)
    per_tile_inj = jnp.take(inj_blocks, tile_bus, axis=1)
    partial_flows = jnp.einsum(
        "stb,tlb->tsl", per_tile_inj, tile_full, preferred_element_type=jnp.float32
    )
    owner_index = tile_line // line_blocks
    within_owner = tile_line % line_blocks
    owner_hits = (owner_index[:, None] == jnp.arange(bus_count, dtype=jnp.int32)[None, :]).astype(
        jnp.int32
    )
    rank_within = jnp.sum(jnp.cumsum(owner_hits, axis=0) * owner_hits, axis=1) - 1
    slot_index = owner_index * capacity + rank_within
    send_buffer = (
        jnp.zeros((slot_total, row_count, tile_size), jnp.float32).at[slot_index].set(partial_flows)
    )
    slot_label = jnp.full((slot_total,), -1, jnp.int32).at[slot_index].set(within_owner)
    received, received_label = (
        lax.all_to_all(send_buffer, "bus", split_axis=0, concat_axis=0, tiled=True),
        lax.all_to_all(slot_label, "bus", split_axis=0, concat_axis=0, tiled=True),
    )
    select_mask = (
        received_label[None, :] == jnp.arange(line_blocks, dtype=jnp.int32)[:, None]
    ).astype(jnp.float32)
    flow_blocks = jnp.einsum("ms,srl->rml", select_mask, received, precision=lax.Precision.HIGHEST)
    flows = flow_blocks.reshape(row_count, line_blocks * tile_size)
    line_cap = line_limit.astype(jnp.float32) * 0.01
    residual = flows - flow_pred.astype(jnp.float32)
    grad_flow = (
        residual
        + jax.nn.sigmoid(4.0 * (flows - line_cap))
        - jax.nn.sigmoid(4.0 * (-flows - line_cap))
    ).astype(jnp.bfloat16)
    gathered = lax.all_gather(grad_flow, "bus", axis=1, tiled=True)
    gathered_blocks = gathered.reshape(row_count, gathered.shape[1] // tile_size, tile_size)
    per_tile_grad = jnp.take(gathered_blocks, tile_line, axis=1)
    contrib = jnp.einsum(
        "stl,tlb->stb", per_tile_grad, tile_full, preferred_element_type=jnp.float32
    )
    bus_select = (tile_bus[:, None] == jnp.arange(blocks_here, dtype=jnp.int32)[None, :]).astype(
        jnp.float32
    )
    grad_blocks_bus = jnp.einsum(
        "stb,tk->skb", contrib, bus_select, precision=lax.Precision.HIGHEST
    )
    grad_local = grad_blocks_bus.reshape(row_count, blocks_here * tile_size).astype(jnp.bfloat16)
    grad_injections = lax.all_to_all(grad_local, "bus", split_axis=0, concat_axis=1, tiled=True)
    return (grad_injections, flows)


def solution(mesh):
    return jax.shard_map(
        per_device,
        mesh=mesh,
        in_specs=(
            P(("scen", "bus"), None),
            P("bus", "scen", None),
            P("bus"),
            P("bus"),
            P("scen", "bus"),
            P("bus"),
        ),
        out_specs=(P(("scen", "bus"), None), P("scen", "bus")),
        check_vma=False,
    )
```

profile of v0, /device:TPU:0, one launch (start us, length us, event | category | flops | bytes accessed | tf_op | source)
XLA Modules:
  0.0 287.0 jit_solution(16097917013080427183)
XLA Ops:
  7.2 0.0 all-gather.3.cloned.1.call-start
  7.2 0.7 all-gather.3.cloned.1.call-update
  7.9 7.4 %all-to-all-start = ((bf16[8,16,256]{2,0,1:T(8,128)(2,1)}), bf16[8,16,256]{2,0,1:T(8,128)(2,1)S(1)}, u32[]{:S(2)}, u32[]{:S(2)}) async-start(bf16[8,16,256]{2,0,1:T(8,128)(2,1)} %bitcast.34), calls=%async_computation | async-start | bytes 131072 | tf_op jit(solution)/shard_map/all_to_all | solution.py:9
  15.3 0.7 compare_select_fusion.2
  16.0 0.1 fusion.22
  16.1 0.1 reduce_window_sum.11
  16.1 0.2 select_reduce_fusion
  16.3 0.7 compare_select_fusion
  17.0 0.7 compare_and_fusion
  17.7 0.8 scatter_custom_fusion.1
  18.4 0.7 all_to_all.37
  19.1 3.1 %all-to-all-done = bf16[8,16,256]{2,0,1:T(8,128)(2,1)S(1)} async-done(((bf16[8,16,256]{2,0,1:T(8,128)(2,1)}), bf16[8,16,256]{2,0,1:T(8,128)(2,1)S(1)}, u32[]{:S(2)}, u32[]{:S(2)}) %all-to-all-start) | async-done | bytes 65568 | tf_op jit(solution)/shard_map/all_to_all | solution.py:9
  22.2 3.5 %all-to-all-start.2 = ((s32[16,6,1]{1,2,0:T(1,128)}), s32[16,6,1]{1,2,0:T(1,128)S(1)}, u32[]{:S(2)}, u32[]{:S(2)}) async-start(s32[16,6,1]{1,2,0:T(1,128)} %bitcast.4), calls=%async_computation.2 | async-start | bytes 16384 | tf_op jit(solution)/shard_map/all_to_all | solution.py:37
  25.7 1.0 gather_fusion
  26.7 18.7 %all-gather.3.cloned.1.call-done = bf16[64,128,128]{2,1,0:T(8,128)(2,1)} async-done(((bf16[64,64,128]{2,1,0:T(8,128)(2,1)}), bf16[64,128,128]{2,1,0:T(8,128)(2,1)}) %all-gather.3.cloned.1.call-update) | async-done | bytes 2097168 | tf_op jit(solution)/shard_map/all_gather | solution.py:10
  45.4 5.2 %fusion.5 = f32[64,128,128]{2,1,0:T(8,128)} fusion(bf16[64,128,128]{2,1,0:T(8,128)(2,1)} %all-gather.3.cloned.1.call-done, bf16[64,128,128]{2,1,0:T(8,128)(2,1)S(1)} %gather_fusion, pred[64]{0:T(512)(128)(4,1)S(1)} %compare_and_fusion), kind=kOutput, calls=%fused_computation.10 | convolution fusion | flops 269484032 | bytes 8388672 | tf_op jit(solution)/shard_map/stb,tlb->tsl/dot_general | solution.py:21
  50.6 3.4 %broadcast_in_dim.41 = f32[96,128,128]{2,1,0:T(8,128)} broadcast(f32[]{:T(128)} %constant.58.clone.1), dimensions={} | broadcast | bytes 6291460 | tf_op jit(solution)/shard_map/broadcast_in_dim | solution.py:32
  54.1 12.0 %scatter_fusion = f32[96,128,128]{2,1,0:T(8,128)} fusion(f32[96,128,128]{2,1,0:T(8,128)} %broadcast_in_dim.41, s32[64]{0:T(128)S(1)} %compare_select_fusion.1, f32[64,128,128]{2,1,0:T(8,128)} %fusion.5), kind=kCustom, calls=%fused_computation.2 | custom fusion | bytes 12583168 | tf_op jit(solution)/shard_map/scatter | solution.py:32
  66.1 0.0 copy-start
  66.1 0.0 copy-start.1
  66.1 0.0 all-to-all-done.2
  66.1 5.8 %all-to-all-start.1 = ((f32[96,128,128]{2,1,0:T(8,128)}), f32[96,128,128]{2,1,0:T(8,128)}, u32[]{:S(2)}, u32[]{:S(2)}) async-start(f32[96,128,128]{2,1,0:T(8,128)} %scatter_fusion), calls=%async_computation.1 | async-start | bytes 12582912 | tf_op jit(solution)/shard_map/all_to_all | solution.py:36
  71.9 0.2 all-gather.5.cloned.1.call-start
  72.1 0.0 copy-done
  72.1 0.1 copy.23
  72.3 0.0 copy-done.1
  72.3 0.5 broadcast.71
  72.8 0.7 reduce.3
  73.5 0.1 eq.49
  73.6 0.0 copy-start.3
  73.6 112.5 %all-to-all-done.1 = f32[96,128,128]{2,1,0:T(8,128)} async-done(((f32[96,128,128]{2,1,0:T(8,128)}), f32[96,128,128]{2,1,0:T(8,128)}, u32[]{:S(2)}, u32[]{:S(2)}) %all-to-all-start.1) | async-done | bytes 6291488 | tf_op jit(solution)/shard_map/all_to_all | solution.py:36
  186.1 8.1 %fusion.11 = f32[128,3,128]{2,1,0:T(4,128)S(1)} fusion(f32[96,128,128]{2,1,0:T(8,128)} %all-to-all-done.1, s32[96]{0:T(128)S(1)} %eq.49), kind=kOutput, calls=%fused_computation.16 | convolution fusion | flops 56623392 | bytes 6488448 | tf_op jit(solution)/shard_map/ms,srl->rml/dot_general | solution.py:42
  194.2 0.1 copy.22
  194.3 0.8 subtract_convert_fusion
  195.1 0.0 all-gather.5.cloned.1.call-update
  195.2 0.0 copy-done.3
  195.2 62.2 %all-gather.5.cloned.1.call-done = bf16[128,6144]{0,1:T(8,128)(2,1)} async-done(((bf16[128,384]{0,1:T(8,128)(2,1)}), bf16[128,6144]{0,1:T(8,128)(2,1)}) %all-gather.5.cloned.1.call-update) | async-done | bytes 1572880 | tf_op jit(solution)/shard_map/all_gather | solution.py:51
  257.4 1.9 copy.24
  259.4 2.2 gather_fusion.1
  261.5 0.0 copy-start.2
  261.5 3.0 %convolution_bitcast_fusion = f32[128,64,128]{2,0,1:T(8,128)S(1)} fusion(bf16[64,128,128]{2,1,0:T(8,128)(2,1)} %all-gather.3.cloned.1.call-done, bf16[64,128,128]{2,1,0:T(8,128)(2,1)} %gather_fusion.1, pred[64]{0:T(512)(128)(4,1)S(1)} %compare_and_fusion.1), kind=kOutput, calls=%fused_computation.8 | convolution fusion | flops 269484032 | bytes 8388672 | tf_op jit(solution)/shard_map/stl,tlb->stb/dot_general | solution.py:54
  264.5 0.0 copy-done.2
  264.5 3.8 %fusion.17 = bf16[128,2,128]{2,1,0:T(2,128)(2,1)S(1)} fusion(f32[128,64,128]{2,0,1:T(8,128)S(1)} %convolution_bitcast_fusion, s32[64]{0:T(128)S(1)} %copy-done.2), kind=kOutput, calls=%fused_computation.18 | convolution fusion | flops 25198720 | bytes 4260096 | tf_op jit(solution)/shard_map/stb,tk->skb/dot_general | solution.py:60
  268.3 0.7 convert_element_type.30
  269.0 3.6 %all-to-all-start.3 = ((bf16[16,8,256]{2,1,0:T(8,128)(2,1)}), bf16[16,8,256]{2,1,0:T(8,128)(2,1)S(1)}, u32[]{:S(2)}, u32[]{:S(2)}) async-start(bf16[16,8,256]{2,1,0:T(8,128)(2,1)} %convert_element_type.30), calls=%async_computation.3 | async-start | bytes 131072 | tf_op jit(solution)/shard_map/all_to_all | solution.py:64
  272.6 0.8 copy.26
  273.4 6.1 %all-to-all-done.3 = bf16[16,8,256]{2,1,0:T(8,128)(2,1)S(1)} async-done(((bf16[16,8,256]{2,1,0:T(8,128)(2,1)}), bf16[16,8,256]{2,1,0:T(8,128)(2,1)S(1)}, u32[]{:S(2)}, u32[]{:S(2)}) %all-to-all-start.3) | async-done | bytes 65568 | tf_op jit(solution)/shard_map/all_to_all | solution.py:64
  279.5 0.6 copy.39
  (7 shorter events, 0.1 us)
Async XLA Ops:
  7.2 38.2 %all-gather.3.cloned.1.call-start = ((), (), s32[]{:S(2)}) async-start(), calls=%async_computation.4 | async-start | bytes 3145728 | tf_op jit(solution)/shard_map/all_gather | solution.py:10
  7.9 14.3 %all-to-all-start = ((bf16[8,16,256]{2,0,1:T(8,128)(2,1)}), bf16[8,16,256]{2,0,1:T(8,128)(2,1)S(1)}, u32[]{:S(2)}, u32[]{:S(2)}) async-start(bf16[8,16,256]{2,0,1:T(8,128)(2,1)} %bitcast.34), calls=%async_computation | async-start | bytes 131072 | tf_op jit(solution)/shard_map/all_to_all | solution.py:9
  22.2 43.9 %all-to-all-start.2 = ((s32[16,6,1]{1,2,0:T(1,128)}), s32[16,6,1]{1,2,0:T(1,128)S(1)}, u32[]{:S(2)}, u32[]{:S(2)}) async-start(s32[16,6,1]{1,2,0:T(1,128)} %bitcast.4), calls=%async_computation.2 | async-start | bytes 16384 | tf_op jit(solution)/shard_map/all_to_all | solution.py:37
  66.1 6.0 %copy-start = (bf16[128,384]{1,0:T(8,128)(2,1)S(1)}, bf16[128,384]{1,0:T(8,128)(2,1)}, u32[]{:S(2)}) copy-start(bf16[128,384]{1,0:T(8,128)(2,1)} %param.10) | copy-start | bytes 294916
  66.1 6.2 %copy-start.1 = (s32[384]{0:T(512)S(1)}, s32[384]{0:T(512)}, u32[]{:S(2)}) copy-start(s32[384]{0:T(512)} %param.11) | copy-start | bytes 4612
  66.1 120.0 %all-to-all-start.1 = ((f32[96,128,128]{2,1,0:T(8,128)}), f32[96,128,128]{2,1,0:T(8,128)}, u32[]{:S(2)}, u32[]{:S(2)}) async-start(f32[96,128,128]{2,1,0:T(8,128)} %scatter_fusion), calls=%async_computation.1 | async-start | bytes 12582912 | tf_op jit(solution)/shard_map/all_to_all | solution.py:36
  71.9 185.6 %all-gather.5.cloned.1.call-start = ((), (), s32[]{:S(2)}) async-start(), calls=%async_computation.5 | async-start | bytes 1671168 | tf_op jit(solution)/shard_map/all_gather | solution.py:51
  73.6 121.6 %copy-start.3 = (s32[64]{0:T(128)S(1)}, s32[64]{0:T(128)}, u32[]{:S(2)}) copy-start(s32[64]{0:T(128)} %param.8) | copy-start | bytes 772
  261.5 3.0 %copy-start.2 = (s32[64]{0:T(128)S(1)}, s32[64]{0:T(128)}, u32[]{:S(2)}) copy-start(s32[64]{0:T(128)} %param.9) | copy-start | bytes 772
  269.0 10.5 %all-to-all-start.3 = ((bf16[16,8,256]{2,1,0:T(8,128)(2,1)}), bf16[16,8,256]{2,1,0:T(8,128)(2,1)S(1)}, u32[]{:S(2)}, u32[]{:S(2)}) async-start(bf16[16,8,256]{2,1,0:T(8,128)(2,1)} %convert_element_type.30), calls=%async_computation.3 | async-start | bytes 131072 | tf_op jit(solution)/shard_map/all_to_all | solution.py:64
Sparse Core Ops, SparseCore 0:
  9.5 35.7 all-gather.2
  195.3 62.1 all-gather.4
where the time goes:
time: 288 us; the launch traced here: 287 us
  waiting for transfers between devices  203 us (70%)
  local copies, waits for them, and re-layouts  25 us (9%)
  starting transfers between devices  20.5 us (7%)
  matrix products  20.1 us (7%)
  between operations  14.2 us (5%)
  other arithmetic  3.88 us (1%)
    all_to_all x1, waiting for transfers between devices, per_device(): lax.all_to_all(send_buffer, 'bus', split_axis=0, concat_axis=0, tiled=True)  113 us
    all_gather x1, waiting for transfers between devices, per_device(): gathered = lax.all_gather(grad_flow, 'bus', axis=1, tiled=True)  62.2 us
    all_gather x1, waiting for transfers between devices, per_device(): tile_full = lax.all_gather(tile_values, 'scen', axis=1, tiled=True)  18.7 us
    scatter x1, local copies, waits for them, and re-layouts, per_device(): jnp.zeros((slot_total, row_count, tile_size), jnp.float32).at[slot_index]  12 us
    dot_general x1, matrix products, per_device(): jnp.einsum('ms,srl->rml', select_mask, received, precision=lax.Precision....  8.08 us
    all_to_all x1, starting transfers between devices, per_device(): lax.all_to_all(injections, 'bus', split_axis=1, concat_axis=0, tiled=True)  7.4 us
    all_to_all x1, waiting for transfers between devices, per_device(): lax.all_to_all(grad_local, 'bus', split_axis=0, concat_axis=1, tiled=True)  6.08 us
    all_to_all x1, starting transfers between devices, per_device(): lax.all_to_all(send_buffer, 'bus', split_axis=0, concat_axis=0, tiled=True)  5.78 us
  transfers between devices with their start and end apart: 6, of which 5 were waited for; matrix products, arithmetic and copies ran while one was open for 9% of the time, Pallas kernels for 0%

commit v1 on v0

--- a/solution.py
+++ b/solution.py
@@ -1,7 +1,359 @@
 import jax
 import jax.numpy as jnp
 from jax import lax
+from jax.experimental import pallas as pl
+from jax.experimental.pallas import tpu as pltpu
 from jax.sharding import PartitionSpec as P
+
+MESH_ID = pl.DeviceIdType.MESH
+F32 = jnp.float32
+BF16 = jnp.bfloat16
+
+
+def kernel(inj_ref, tiles_ref, line_ref, busid_ref, pred_ref, lim_ref, gout_ref, fout_ref,
+           table_v, table_s, inj_buf, inj_t, dense, dense_t,
+           csend, crecv, ysend, yrecv, acc, zsend, zrecv,
+           pred_recv, pred_t, fx_send, fx_recv, fx_own,
+           ag, gx_send, gx_own, gx_recv, gsend, grecv,
+           table_sem, inj_ss, inj_rs, pred_sem, c_ss, c_rs, y_ss, y_rs, z_ss, z_rs,
+           fx_sem, az_ss, az_rs, ay_ss, ay_rs, ac_ss, ac_rs, gx_sem, out_ss, out_rs):
+    s = lax.axis_index("scen")
+    b = lax.axis_index("bus")
+    c = b % 2
+    y = (b // 2) % 2
+    z = b // 4
+    me = s * 16 + b
+    core_mate = (s, b + 1 - 2 * c)
+    y_mate = (s, b + 2 - 4 * y)
+    x_mate = (1 - s, b)
+
+    def zdev(i):
+        return (s, ((z + 1 + i) % 4) * 4 + y * 2 + c)
+
+    def copy(src, dst, ss, rs, dev):
+        return pltpu.make_async_remote_copy(
+            src_ref=src, dst_ref=dst, send_sem=ss, recv_sem=rs,
+            device_id=dev, device_id_type=MESH_ID)
+
+    barrier = pltpu.get_barrier_semaphore()
+
+    def greet(k, carry):
+        d = (me + k) % 32
+        pl.semaphore_signal(barrier, inc=1, device_id=(d // 16, d % 16), device_id_type=MESH_ID)
+        return carry
+
+    lax.fori_loop(1, 32, greet, 0)
+
+    row = line_ref[...]
+    sub = lax.broadcasted_iota(jnp.int32, (64, 64), 0)
+    lane = lax.broadcasted_iota(jnp.int32, (64, 64), 1)
+    rows = jnp.broadcast_to(row, (64, 64))
+    diag = sub == lane
+    col = jnp.sum(jnp.where(diag, rows, 0), axis=1, keepdims=True)
+    bus_col = jnp.sum(jnp.where(diag, jnp.broadcast_to(busid_ref[...], (64, 64)), 0), axis=1, keepdims=True)
+    owner_row = rows // 3
+    owner_col = col // 3
+    same = jnp.where((owner_row == owner_col) & (lane < sub), 1, 0)
+    rank = jnp.sum(same, axis=1, keepdims=True)
+    place = owner_col * 6 + rank
+    tcol = lax.broadcasted_iota(jnp.int32, (64, 1), 0)
+    code = tcol * 8 + (col - owner_col * 3 + 1) * 2 + bus_col
+    slot_ids = lax.broadcasted_iota(jnp.int32, (64, 128), 1)
+    table = jnp.sum(jnp.where(place == slot_ids, code, 0), axis=0, keepdims=True)
+    table_v[...] = jnp.broadcast_to(table, (8, 128))
+    to_smem = pltpu.make_async_copy(table_v, table_s, table_sem)
+    to_smem.start()
+    pl.semaphore_wait(barrier, 31)
+
+    def inj_copy(k):
+        d = (me + k) % 32
+        src = (me + 32 - k) % 32
+        db = d % 16
+        out = copy(inj_ref.at[:, pl.ds(pl.multiple_of(db * 256, 256), 256)],
+                   inj_buf.at[me], inj_ss.at[k], inj_rs.at[k], (d // 16, db))
+        inn = copy(inj_ref.at[:, pl.ds(pl.multiple_of(db * 256, 256), 256)],
+                   inj_buf.at[src], inj_ss.at[k], inj_rs.at[k], (d // 16, db))
+        return out, inn
+
+    def inj_start(k, carry):
+        inj_copy(k)[0].start()
+        return carry
+
+    lax.fori_loop(1, 32, inj_start, 0)
+    pred_copy = copy(pred_ref, pred_recv, pred_sem.at[0], pred_sem.at[1], x_mate)
+    pred_copy.start()
+    inj_buf[me] = inj_ref[:, pl.ds(pl.multiple_of(b * 256, 256), 256)]
+
+    to_smem.wait()
+
+    def build(o, carry):
+        tiles = []
+        for j in range(6):
+            v = table_s[0, o * 6 + j]
+            tiles.append((tiles_ref[v // 8].astype(F32), (v // 2) % 4, v % 2))
+        for m in range(3):
+            for bb in range(2):
+                total = jnp.zeros((64, 128), F32)
+                for tile, blk, bus in tiles:
+                    w = jnp.where((blk == m + 1) & (bus == bb), 1.0, 0.0).astype(F32)
+                    total = total + tile * w
+                hi = total.astype(BF16)
+                lo = (total - hi.astype(F32)).astype(BF16)
+                dense[o, 0, pl.ds(m * 64, 64), pl.ds(bb * 128, 128)] = hi
+                dense[o, 1, pl.ds(m * 64, 64), pl.ds(bb * 128, 128)] = lo
+        return carry
+
+    lax.fori_loop(0, 16, build, 0)
+
+    def inj_wait(k, carry):
+        inj_copy(k)[1].wait_recv()
+        return carry
+
+    lax.fori_loop(1, 32, inj_wait, 0)
+    inj_t[...] = inj_buf[...].astype(F32).reshape(256, 256).T.astype(BF16)
+
+    def forward(o):
+        return (jnp.dot(dense[o, 0], inj_t[...], preferred_element_type=F32)
+                + jnp.dot(dense[o, 1], inj_t[...], preferred_element_type=F32))
+
+    def owner(k, core):
+        far = k // 4
+        zz = (z + 1 + k % 4) % 4
+        yy = jnp.where(far == 0, 1 - y, y)
+        return zz * 4 + yy * 2 + core
+
+    def c_copy(k):
+        return copy(csend.at[k], crecv.at[k], c_ss.at[k], c_rs.at[k], core_mate)
+
+    def y_copy(k):
+        return copy(ysend.at[k], yrecv.at[k], y_ss.at[k], y_rs.at[k], y_mate)
+
+    def z_copy(i):
+        return copy(zsend.at[i], zrecv.at[2 - i], z_ss.at[i], z_rs.at[2 - i], zdev(i))
+
+    def z_arrival(j):
+        return copy(zsend.at[j], zrecv.at[j], z_ss.at[j], z_rs.at[j], zdev(j))
+
+    def send_core(k, carry):
+        csend[k] = forward(owner(k, 1 - c)).astype(BF16)
+        c_copy(k).start()
+        return carry
+
+    lax.fori_loop(0, 8, send_core, 0)
+
+    def send_y(k, carry):
+        part = forward(owner(k, c))
+        c_copy(k).wait_recv()
+        ysend[k] = (part + crecv[k].astype(F32)).astype(BF16)
+        y_copy(k).start()
+        return carry
+
+    lax.fori_loop(0, 4, send_y, 0)
+
+    def keep(k, carry):
+        part = forward(owner(k, c))
+        c_copy(k).wait_recv()
+        acc[k - 4] = part + crecv[k].astype(F32)
+        return carry
+
+    lax.fori_loop(4, 8, keep, 0)
+    pred_copy.wait_recv()
+    mine = pred_ref[...].astype(F32).T
+    theirs = pred_recv[...].astype(F32).T
+    lim_all = jnp.broadcast_to(lim_ref[...].astype(F32) * 0.01, (128, 384)).T
+    first = s == 0
+    for m in range(3):
+        upper, lower = slice(m * 128, m * 128 + 64), slice(m * 128 + 64, m * 128 + 128)
+        a = jnp.where(first, mine[upper], mine[lower])
+        d = jnp.where(first, theirs[upper], theirs[lower])
+        pred_t[0, pl.ds(m * 64, 64), pl.ds(0, 128)] = jnp.where(first, a, d)
+        pred_t[0, pl.ds(m * 64, 64), pl.ds(128, 128)] = jnp.where(first, d, a)
+        e = jnp.where(first, lim_all[upper], lim_all[lower])
+        pred_t[1, pl.ds(m * 64, 64), pl.ds(0, 128)] = e
+        pred_t[1, pl.ds(m * 64, 64), pl.ds(128, 128)] = e
+
+    for i in range(3):
+        y_copy(i).wait_recv()
+        zsend[i] = (acc[i] + yrecv[i].astype(F32)).astype(BF16)
+        z_copy(i).start()
+
+    def turn(o, carry):
+        dense_t[o, 0] = dense[o, 0].T
+        dense_t[o, 1] = dense[o, 1].T
+        return carry
+
+    lax.fori_loop(0, 16, turn, 0)
+    y_copy(3).wait_recv()
+    flow = acc[3] + yrecv[3].astype(F32)
+    for j in range(3):
+        z_arrival(j).wait_recv()
+        flow = flow + zrecv[j].astype(F32)
+
+    limit = pred_t[1]
+    grad = ((flow - pred_t[0]) + jax.nn.sigmoid(4.0 * (flow - limit))
+            - jax.nn.sigmoid(4.0 * (-flow - limit)))
+    ag[3] = grad.astype(BF16)
+
+    def az_copy(i):
+        return copy(ag.at[3], ag.at[2 - i], az_ss.at[i], az_rs.at[2 - i], zdev(i))
+
+    def az_arrival(j):
+        return copy(ag.at[3], ag.at[j], az_ss.at[j], az_rs.at[j], zdev(j))
+
+    def ay_copy(i):
+        return copy(ag.at[i], ag.at[4 + i], ay_ss.at[i], ay_rs.at[i], y_mate)
+
+    def ac_copy(i):
+        return copy(ag.at[i], ag.at[8 + i], ac_ss.at[i], ac_rs.at[i], core_mate)
+
+    for i in range(3):
+        az_copy(i).start()
+    ay_copy(3).start()
+    ac_copy(3).start()
+    fx_send[...] = jnp.where(first, flow[:, 128:], flow[:, :128])
+    fx_own[...] = jnp.where(first, flow[:, :128], flow[:, 128:])
+    fx_copy = copy(fx_send, fx_recv, fx_sem.at[0], fx_sem.at[1], x_mate)
+    fx_copy.start()
+
+    def backward(slot):
+        zz = (z + 1 + slot % 4) % 4
+        yy = (y + slot // 4) % 2
+        cc = (c + slot // 8) % 2
+        o = zz * 4 + yy * 2 + cc
+        return (jnp.dot(dense_t[o, 0], ag[slot], preferred_element_type=F32)
+                + jnp.dot(dense_t[o, 1], ag[slot], preferred_element_type=F32))
+
+    total = gx_own
+    total[...] = backward(3)
+
+    for i in range(3):
+        az_arrival(i).wait_recv()
+        ay_copy(i).start()
+        ac_copy(i).start()
+        total[...] += backward(i)
+    for i in (3, 0, 1, 2):
+        ay_copy(i).wait_recv()
+        ac_copy(4 + i).start()
+        total[...] += backward(4 + i)
+    for i in (3, 0, 1, 2, 7, 4, 5, 6):
+        ac_copy(i).wait_recv()
+        total[...] += backward(8 + i)
+
+    whole = total[...]
+    gx_send[...] = jnp.where(first, whole[:, 128:], whole[:, :128])
+    gx_copy = copy(gx_send, gx_recv, gx_sem.at[0], gx_sem.at[1], x_mate)
+    gx_copy.start()
+
+    fx_copy.wait_recv()
+    for m in range(3):
+        rows_m = pl.ds(m * 64, 64)
+        mine_m, other_m = fx_own[rows_m, :], fx_recv[rows_m, :]
+        top = jnp.where(first, mine_m, other_m)
+        low = jnp.where(first, other_m, mine_m)
+        fout_ref[:, pl.ds(m * 128, 128)] = jnp.concatenate([top, low], axis=0).T
+
+    kept = jnp.where(first, whole[:, :128], whole[:, 128:])
+    gx_copy.wait_recv()
+    gsend[...] = (kept + gx_recv[...]).T.reshape(16, 8, 256).astype(BF16)
+
+    def out_copy(k):
+        d = (b + k) % 16
+        src = (b + 16 - k) % 16
+        out = copy(gsend.at[d], grecv.at[b], out_ss.at[k], out_rs.at[k], (s, d))
+        inn = copy(gsend.at[d], grecv.at[src], out_ss.at[k], out_rs.at[k], (s, d))
+        return out, inn
+
+    def out_start(k, carry):
+        out_copy(k)[0].start()
+        return carry
+
+    lax.fori_loop(1, 16, out_start, 0)
+    grecv[b] = gsend[b]
+
+    def sent_inj(k, carry):
+        inj_copy(k)[0].wait_send()
+        return carry
+
+    lax.fori_loop(1, 32, sent_inj, 0)
+
+    def sent_c(k, carry):
+        c_copy(k).wait_send()
+        ac_copy(k).wait_send()
+        return carry
+
+    lax.fori_loop(0, 8, sent_c, 0)
+
+    def sent_y(k, carry):
+        y_copy(k).wait_send()
+        ay_copy(k).wait_send()
+        return carry
+
+    lax.fori_loop(0, 4, sent_y, 0)
+    for i in range(3):
+        z_copy(i).wait_send()
+        az_copy(i).wait_send()
+    pred_copy.wait_send()
+    fx_copy.wait_send()
+    gx_copy.wait_send()
+
+    def out_wait(k, carry):
+        out_copy(k)[1].wait_recv()
+        return carry
+
+    lax.fori_loop(1, 16, out_wait, 0)
+    for k in range(16):
+        gout_ref[:, pl.ds(k * 256, 256)] = grecv[k]
+
+    def sent_out(k, carry):
+        out_copy(k)[0].wait_send()
+        return carry
+
+    lax.fori_loop(1, 16, sent_out, 0)
+
+
+def fused(injections, tile_values, tile_line, tile_bus, flow_pred, line_limit):
+    vmem = pl.BlockSpec(memory_space=pltpu.VMEM)
+    dma = pltpu.SemaphoreType.DMA
+    block = (192, 256)
+    return pl.pallas_call(
+        kernel,
+        out_shape=(jax.ShapeDtypeStruct((8, 4096), BF16), jax.ShapeDtypeStruct((128, 384), F32)),
+        in_specs=[vmem] * 6,
+        out_specs=(vmem, vmem),
+        scratch_shapes=[
+            pltpu.VMEM((8, 128), jnp.int32),
+            pltpu.SMEM((8, 128), jnp.int32),
+            pltpu.VMEM((32, 8, 256), BF16),
+            pltpu.VMEM((256, 256), BF16),
+            pltpu.VMEM((16, 2) + block, BF16),
+            pltpu.VMEM((16, 2, 256, 192), BF16),
+            pltpu.VMEM((8,) + block, BF16),
+            pltpu.VMEM((8,) + block, BF16),
+            pltpu.VMEM((4,) + block, BF16),
+            pltpu.VMEM((4,) + block, BF16),
+            pltpu.VMEM((4,) + block, F32),
+            pltpu.VMEM((3,) + block, BF16),
+            pltpu.VMEM((3,) + block, BF16),
+            pltpu.VMEM((128, 384), BF16),
+            pltpu.VMEM((2,) + block, F32),
+            pltpu.VMEM((192, 128), F32),
+            pltpu.VMEM((192, 128), F32),
+            pltpu.VMEM((192, 128), F32),
+            pltpu.VMEM((16,) + block, BF16),
+            pltpu.VMEM((256, 128), F32),
+            pltpu.VMEM((256, 256), F32),
+            pltpu.VMEM((256, 128), F32),
+            pltpu.VMEM((16, 8, 256), BF16),
+            pltpu.VMEM((16, 8, 256), BF16),
+            dma, dma((32,)), dma((32,)), dma((2,)),
+            dma((8,)), dma((8,)), dma((4,)), dma((4,)), dma((3,)), dma((3,)),
+            dma((2,)), dma((3,)), dma((3,)), dma((4,)), dma((4,)), dma((8,)), dma((8,)),
+            dma((2,)), dma((16,)), dma((16,)),
+        ],
+        compiler_params=pltpu.CompilerParams(
+            collective_id=0, has_side_effects=True, vmem_limit_bytes=48 * 1024 * 1024),
+    )(injections, tile_values, tile_line.reshape(1, -1), tile_bus.reshape(1, -1), flow_pred,
+      line_limit.reshape(1, -1))
 
 
 def per_device(injections, tile_values, tile_line, tile_bus, flow_pred, line_limit):
@@ -66,8 +418,9 @@
 
 
 def solution(mesh):
+    small = mesh.shape["scen"] == 2 and mesh.shape["bus"] == 16
     return jax.shard_map(
-        per_device,
+        fused if small else per_device,
         mesh=mesh,
         in_specs=(
             P(("scen", "bus"), None),

time: 288 us -> 63.4 us (0.22)
  waiting for transfers between devices: 203 us -> 0 us
  Pallas kernels: 0 us -> 56.9 us
  starting transfers between devices: 20.5 us -> 0 us
  matrix products: 20.1 us -> 0 us
  local copies, waits for them, and re-layouts: 25 us -> 5.61 us
  between operations: 14.2 us -> 0.65 us
  other arithmetic: 3.88 us -> 0 us
    all_to_all x4 -> x0, waiting for transfers between devices: 122 us -> none  [the longest x1 113 us: per_device(): lax.all_to_all(send_buffer, 'bus', split_axis=0, concat_axis=0, tiled=True)]
    all_gather x2 -> x0, waiting for transfers between devices: 80.9 us -> none  [the longest x1 62.2 us: per_device(): gathered = lax.all_gather(grad_flow, 'bus', axis=1, tiled=True)]
    pallas_call x0 -> x1, Pallas kernels: none -> 56.9 us  [fused(): pl.pallas_call(kernel, out_shape=(jax.ShapeDtypeStruct((8, 4096), BF16),...]
    all_to_all x4 -> x0, starting transfers between devices: 20.2 us -> none  [the longest x1 7.4 us: per_device(): lax.all_to_all(injections, 'bus', split_axis=1, concat_axis=0, tiled=True)]
    dot_general x4 -> x0, matrix products: 20.1 us -> none  [the longest x1 8.08 us: per_device(): jnp.einsum('ms,srl->rml', select_mask, received, precision=lax.Precision....]
    scatter x2 -> x0, local copies, waits for them, and re-layouts: 12.8 us -> none  [the longest x1 12 us: per_device(): jnp.zeros((slot_total, row_count, tile_size), jnp.float32).at[slot_index]]
    unnamed x11 -> x14, local copies, waits for them, and re-layouts: 1.58 us -> 5.61 us
    broadcast_in_dim x1 -> x0, local copies, waits for them, and re-layouts: 3.45 us -> none  [per_device(): jnp.zeros((slot_total, row_count, tile_size), jnp.float32).at[slot_index]]
  transfers between devices with their start and end apart: 6 -> 0, of which waited for: 5 -> 0; matrix products, arithmetic and copies ran while one was open for 9% -> 0% of each run, Pallas kernels for 0% -> 0%
where the time goes in v1:
time: 63.4 us; the launch traced here: 63.1 us
  Pallas kernels  56.9 us (90%)
  local copies, waits for them, and re-layouts  5.61 us (9%)
  between operations  0.65 us (1%)
    pallas_call x1, Pallas kernels, fused(): pl.pallas_call(kernel, out_shape=(jax.ShapeDtypeStruct((8, 4096), BF16),...  56.9 us
    unnamed x14, local copies, waits for them, and re-layouts  5.61 us

profile of v1, /device:TPU:0, one launch (start us, length us, event | category | flops | bytes accessed | tf_op | source)
XLA Modules:
  0.0 63.1 jit_solution(73173915170594962)
XLA Ops:
  0.6 0.0 copy-start.5
  0.6 0.7 %copy-done.5 = s32[384]{0:T(512)S(1)} copy-done((s32[384]{0:T(512)S(1)}, s32[384]{0:T(512)}, u32[]{:S(2)}) %copy-start.5) | copy-done | bytes 1560
  1.3 0.0 copy-start.3
  1.3 0.0 copy-start.4
  1.3 0.6 %copy-done.3 = s32[64]{0:T(128)S(1)} copy-done((s32[64]{0:T(128)S(1)}, s32[64]{0:T(128)}, u32[]{:S(2)}) %copy-start.3) | copy-done | bytes 280
  2.0 0.0 copy-done.4
  2.0 0.0 copy-start
  2.0 1.2 %copy-done = bf16[64,64,128]{2,1,0:T(8,128)(2,1)S(1)} copy-done((bf16[64,64,128]{2,1,0:T(8,128)(2,1)S(1)}, bf16[64,64,128]{2,1,0:T(8,128)(2,1)}, u32[]{:S(2)}) %copy-start) | copy-done | bytes 1048600
  3.2 0.0 copy-start.1
  3.2 0.9 %copy-done.1 = bf16[128,384]{1,0:T(8,128)(2,1)S(1)} copy-done((bf16[128,384]{1,0:T(8,128)(2,1)S(1)}, bf16[128,384]{1,0:T(8,128)(2,1)}, u32[]{:S(2)}) %copy-start.1) | copy-done | bytes 98328
  4.1 0.0 copy-start.2
  4.1 0.8 %copy-done.2 = bf16[8,4096]{1,0:T(8,128)(2,1)S(1)} copy-done((bf16[8,4096]{1,0:T(8,128)(2,1)S(1)}, bf16[8,4096]{1,0:T(8,128)(2,1)}, u32[]{:S(2)}) %copy-start.2) | copy-done | bytes 65560
  4.9 56.9 %shard_map.77 = (bf16[8,4096]{1,0:T(8,128)(2,1)S(1)}, f32[128,384]{1,0:T(8,128)S(1)}) custom-call(bf16[8,4096]{1,0:T(8,128)(2,1)S(1)} %copy-done.2, bf16[64,64,128]{2,1,0:T(8,128)(2,1)S(1)} %copy-done, s32[1,64]{1,0:T(1,128)S(1)} %bitcast.2, s32[1,64]{1,0:T(1,128)S(1)} %bitcast.3, bf16[128,384]{1,0:T(8,128)(2,1)S(1)} %copy-done.1, s32[1,384]{1,0:T(1,128)S(1)} %reshape.15.lim_ref), custom_call_target="tpu_custom_call" | custom-call | tf_op jit(solution)/shard_map/pallas_call | solution.py:318
  61.8 0.6 %copy.10 = bf16[8,4096]{1,0:T(8,128)(2,1)} copy(bf16[8,4096]{1,0:T(8,128)(2,1)S(1)} %get-tuple-element.4) | data formatting | bytes 131072
  62.4 0.7 %copy.11 = f32[128,384]{1,0:T(8,128)} copy(f32[128,384]{1,0:T(8,128)S(1)} %get-tuple-element.5) | data formatting | bytes 393216
  (1 shorter events, 0.0 us)
Async XLA Ops:
  0.6 0.7 %copy-start.5 = (s32[384]{0:T(512)S(1)}, s32[384]{0:T(512)}, u32[]{:S(2)}) copy-start(s32[384]{0:T(512)} %param.11) | copy-start | bytes 4612
  1.3 0.7 %copy-start.3 = (s32[64]{0:T(128)S(1)}, s32[64]{0:T(128)}, u32[]{:S(2)}) copy-start(s32[64]{0:T(128)} %param.8) | copy-start | bytes 772
  1.3 0.7 %copy-start.4 = (s32[64]{0:T(128)S(1)}, s32[64]{0:T(128)}, u32[]{:S(2)}) copy-start(s32[64]{0:T(128)} %param.9) | copy-start | bytes 772
  2.0 1.2 %copy-start = (bf16[64,64,128]{2,1,0:T(8,128)(2,1)S(1)}, bf16[64,64,128]{2,1,0:T(8,128)(2,1)}, u32[]{:S(2)}) copy-start(bf16[64,64,128]{2,1,0:T(8,128)(2,1)} %tiles_ref.1) | copy-start | bytes 3145732
  3.2 0.9 %copy-start.1 = (bf16[128,384]{1,0:T(8,128)(2,1)S(1)}, bf16[128,384]{1,0:T(8,128)(2,1)}, u32[]{:S(2)}) copy-start(bf16[128,384]{1,0:T(8,128)(2,1)} %pred_ref.1) | copy-start | bytes 294916
  4.1 0.8 %copy-start.2 = (bf16[8,4096]{1,0:T(8,128)(2,1)S(1)}, bf16[8,4096]{1,0:T(8,128)(2,1)}, u32[]{:S(2)}) copy-start(bf16[8,4096]{1,0:T(8,128)(2,1)} %inj_ref.1) | copy-start | bytes 196612

commit v2 on v1

--- a/solution.py
+++ b/solution.py
@@ -10,12 +10,13 @@
 BF16 = jnp.bfloat16
 
 
-def kernel(inj_ref, tiles_ref, line_ref, busid_ref, pred_ref, lim_ref, gout_ref, fout_ref,
+def kernel(inj_hbm, tiles_hbm, line_hbm, busid_hbm, pred_hbm, lim_hbm, gout_ref, fout_ref,
+           inj_ref, tiles_ref, line_ref, busid_ref, pred_ref, lim_ref,
            table_v, table_s, inj_buf, inj_t, dense, dense_t,
-           csend, crecv, ysend, yrecv, acc, zsend, zrecv,
-           pred_recv, pred_t, fx_send, fx_recv, fx_own,
-           ag, gx_send, gx_own, gx_recv, gsend, grecv,
-           table_sem, inj_ss, inj_rs, pred_sem, c_ss, c_rs, y_ss, y_rs, z_ss, z_rs,
+           csend, crecv, ysend, yrecv, stash, acc, zsend, zrecv,
+           pred_recv, pred_t, flow_t, fx_recv,
+           ag, total, gx_recv, gsend, grecv,
+           in_sem, table_sem, inj_ss, inj_rs, pred_sem, c_ss, c_rs, y_ss, y_rs, z_ss, z_rs,
            fx_sem, az_ss, az_rs, ay_ss, ay_rs, ac_ss, ac_rs, gx_sem, out_ss, out_rs):
     s = lax.axis_index("scen")
     b = lax.axis_index("bus")
@@ -26,6 +27,13 @@
     core_mate = (s, b + 1 - 2 * c)
     y_mate = (s, b + 2 - 4 * y)
     x_mate = (1 - s, b)
+    first = s == 0
+
+    loads = [pltpu.make_async_copy(src, dst, in_sem.at[n]) for n, (src, dst) in enumerate((
+        (line_hbm, line_ref), (busid_hbm, busid_ref), (tiles_hbm, tiles_ref),
+        (inj_hbm, inj_ref), (pred_hbm, pred_ref), (lim_hbm, lim_ref)))]
+    for load in loads:
+        load.start()
 
     def zdev(i):
         return (s, ((z + 1 + i) % 4) * 4 + y * 2 + c)
@@ -44,6 +52,8 @@
 
     lax.fori_loop(1, 32, greet, 0)
 
+    loads[0].wait()
+    loads[1].wait()
     row = line_ref[...]
     sub = lax.broadcasted_iota(jnp.int32, (64, 64), 0)
     lane = lax.broadcasted_iota(jnp.int32, (64, 64), 1)
@@ -69,9 +79,9 @@
         d = (me + k) % 32
         src = (me + 32 - k) % 32
         db = d % 16
-        out = copy(inj_ref.at[:, pl.ds(pl.multiple_of(db * 256, 256), 256)],
+        out = copy(inj_hbm.at[:, pl.ds(pl.multiple_of(db * 256, 256), 256)],
                    inj_buf.at[me], inj_ss.at[k], inj_rs.at[k], (d // 16, db))
-        inn = copy(inj_ref.at[:, pl.ds(pl.multiple_of(db * 256, 256), 256)],
+        inn = copy(inj_hbm.at[:, pl.ds(pl.multiple_of(db * 256, 256), 256)],
                    inj_buf.at[src], inj_ss.at[k], inj_rs.at[k], (d // 16, db))
         return out, inn
 
@@ -80,11 +90,13 @@
         return carry
 
     lax.fori_loop(1, 32, inj_start, 0)
-    pred_copy = copy(pred_ref, pred_recv, pred_sem.at[0], pred_sem.at[1], x_mate)
+    pred_copy = copy(pred_hbm, pred_recv, pred_sem.at[0], pred_sem.at[1], x_mate)
     pred_copy.start()
+    loads[3].wait()
     inj_buf[me] = inj_ref[:, pl.ds(pl.multiple_of(b * 256, 256), 256)]
 
     to_smem.wait()
+    loads[2].wait()
 
     def build(o, carry):
         tiles = []
@@ -110,7 +122,8 @@
         return carry
 
     lax.fori_loop(1, 32, inj_wait, 0)
-    inj_t[...] = inj_buf[...].astype(F32).reshape(256, 256).T.astype(BF16)
+    turned = inj_buf[...].astype(F32).reshape(256, 256).T.astype(BF16)
+    inj_t[...] = jnp.where(first, jnp.concatenate([turned[:, 128:], turned[:, :128]], axis=1), turned)
 
     def forward(o):
         return (jnp.dot(dense[o, 0], inj_t[...], preferred_element_type=F32)
@@ -122,139 +135,153 @@
         yy = jnp.where(far == 0, 1 - y, y)
         return zz * 4 + yy * 2 + core
 
-    def c_copy(k):
-        return copy(csend.at[k], crecv.at[k], c_ss.at[k], c_rs.at[k], core_mate)
-
-    def y_copy(k):
-        return copy(ysend.at[k], yrecv.at[k], y_ss.at[k], y_rs.at[k], y_mate)
-
-    def z_copy(i):
-        return copy(zsend.at[i], zrecv.at[2 - i], z_ss.at[i], z_rs.at[2 - i], zdev(i))
-
-    def z_arrival(j):
-        return copy(zsend.at[j], zrecv.at[j], z_ss.at[j], z_rs.at[j], zdev(j))
+    def c_copy(h, k):
+        return copy(csend.at[h, k], crecv.at[h, k], c_ss.at[h, k], c_rs.at[h, k], core_mate)
+
+    def y_copy(h, k):
+        return copy(ysend.at[h, k], yrecv.at[h, k], y_ss.at[h, k], y_rs.at[h, k], y_mate)
+
+    def z_copy(h, i):
+        return copy(zsend.at[h, i], zrecv.at[h, 2 - i], z_ss.at[h, i], z_rs.at[h, 2 - i], zdev(i))
+
+    def z_arrival(h, j):
+        return copy(zsend.at[h, j], zrecv.at[h, j], z_ss.at[h, j], z_rs.at[h, j], zdev(j))
 
     def send_core(k, carry):
-        csend[k] = forward(owner(k, 1 - c)).astype(BF16)
-        c_copy(k).start()
-        return carry
-
-    lax.fori_loop(0, 8, send_core, 0)
+        part = forward(owner(k, 1 - c)).astype(BF16)
+        csend[0, k] = part[:, :128]
+        c_copy(0, k).start()
+        csend[1, k] = part[:, 128:]
+        c_copy(1, k).start()
+        return carry
 
     def send_y(k, carry):
         part = forward(owner(k, c))
-        c_copy(k).wait_recv()
-        ysend[k] = (part + crecv[k].astype(F32)).astype(BF16)
-        y_copy(k).start()
-        return carry
-
-    lax.fori_loop(0, 4, send_y, 0)
+        stash[k] = part[:, 128:]
+        c_copy(0, k).wait_recv()
+        ysend[0, k] = (part[:, :128] + crecv[0, k].astype(F32)).astype(BF16)
+        y_copy(0, k).start()
+        return carry
+
+    def send_y_late(k, carry):
+        c_copy(1, k).wait_recv()
+        ysend[1, k] = (stash[k] + crecv[1, k].astype(F32)).astype(BF16)
+        y_copy(1, k).start()
+        return carry
 
     def keep(k, carry):
         part = forward(owner(k, c))
-        c_copy(k).wait_recv()
-        acc[k - 4] = part + crecv[k].astype(F32)
-        return carry
-
+        c_copy(0, k).wait_recv()
+        acc[0, k - 4] = part[:, :128] + crecv[0, k].astype(F32)
+        c_copy(1, k).wait_recv()
+        acc[1, k - 4] = part[:, 128:] + crecv[1, k].astype(F32)
+        return carry
+
+    def turn(o, carry):
+        dense_t[o, 0] = dense[o, 0].T
+        dense_t[o, 1] = dense[o, 1].T
+        return carry
+
+    def send_z(h):
+        for i in range(3):
+            y_copy(h, i).wait_recv()
+            zsend[h, i] = (acc[h, i] + yrecv[h, i].astype(F32)).astype(BF16)
+            z_copy(h, i).start()
+
+    lax.fori_loop(0, 4, send_core, 0)
+    lax.fori_loop(0, 4, send_y, 0)
+    lax.fori_loop(4, 8, send_core, 0)
+    lax.fori_loop(0, 4, send_y_late, 0)
     lax.fori_loop(4, 8, keep, 0)
+    send_z(0)
+    loads[4].wait()
+    loads[5].wait()
     pred_copy.wait_recv()
     mine = pred_ref[...].astype(F32).T
     theirs = pred_recv[...].astype(F32).T
     lim_all = jnp.broadcast_to(lim_ref[...].astype(F32) * 0.01, (128, 384)).T
-    first = s == 0
     for m in range(3):
         upper, lower = slice(m * 128, m * 128 + 64), slice(m * 128 + 64, m * 128 + 128)
-        a = jnp.where(first, mine[upper], mine[lower])
-        d = jnp.where(first, theirs[upper], theirs[lower])
-        pred_t[0, pl.ds(m * 64, 64), pl.ds(0, 128)] = jnp.where(first, a, d)
-        pred_t[0, pl.ds(m * 64, 64), pl.ds(128, 128)] = jnp.where(first, d, a)
-        e = jnp.where(first, lim_all[upper], lim_all[lower])
-        pred_t[1, pl.ds(m * 64, 64), pl.ds(0, 128)] = e
-        pred_t[1, pl.ds(m * 64, 64), pl.ds(128, 128)] = e
-
-    for i in range(3):
-        y_copy(i).wait_recv()
-        zsend[i] = (acc[i] + yrecv[i].astype(F32)).astype(BF16)
-        z_copy(i).start()
-
-    def turn(o, carry):
-        dense_t[o, 0] = dense[o, 0].T
-        dense_t[o, 1] = dense[o, 1].T
-        return carry
-
+        for n, array in enumerate((theirs, mine, lim_all)):
+            pred_t[n, pl.ds(m * 64, 64), :] = jnp.where(first, array[upper], array[lower])
+    send_z(1)
     lax.fori_loop(0, 16, turn, 0)
-    y_copy(3).wait_recv()
-    flow = acc[3] + yrecv[3].astype(F32)
-    for j in range(3):
-        z_arrival(j).wait_recv()
-        flow = flow + zrecv[j].astype(F32)
-
-    limit = pred_t[1]
-    grad = ((flow - pred_t[0]) + jax.nn.sigmoid(4.0 * (flow - limit))
-            - jax.nn.sigmoid(4.0 * (-flow - limit)))
-    ag[3] = grad.astype(BF16)
-
-    def az_copy(i):
-        return copy(ag.at[3], ag.at[2 - i], az_ss.at[i], az_rs.at[2 - i], zdev(i))
-
-    def az_arrival(j):
-        return copy(ag.at[3], ag.at[j], az_ss.at[j], az_rs.at[j], zdev(j))
-
-    def ay_copy(i):
-        return copy(ag.at[i], ag.at[4 + i], ay_ss.at[i], ay_rs.at[i], y_mate)
-
-    def ac_copy(i):
-        return copy(ag.at[i], ag.at[8 + i], ac_ss.at[i], ac_rs.at[i], core_mate)
-
-    for i in range(3):
-        az_copy(i).start()
-    ay_copy(3).start()
-    ac_copy(3).start()
-    fx_send[...] = jnp.where(first, flow[:, 128:], flow[:, :128])
-    fx_own[...] = jnp.where(first, flow[:, :128], flow[:, 128:])
-    fx_copy = copy(fx_send, fx_recv, fx_sem.at[0], fx_sem.at[1], x_mate)
-    fx_copy.start()
-
-    def backward(slot):
+
+    def az_copy(h, i):
+        return copy(ag.at[h, 3], ag.at[h, 2 - i], az_ss.at[h, i], az_rs.at[h, 2 - i], zdev(i))
+
+    def az_arrival(h, j):
+        return copy(ag.at[h, 3], ag.at[h, j], az_ss.at[h, j], az_rs.at[h, j], zdev(j))
+
+    def ay_copy(h, i):
+        return copy(ag.at[h, i], ag.at[h, 4 + i], ay_ss.at[h, i], ay_rs.at[h, i], y_mate)
+
+    def ac_copy(h, i):
+        return copy(ag.at[h, i], ag.at[h, 8 + i], ac_ss.at[h, i], ac_rs.at[h, i], core_mate)
+
+    def finish(h):
+        y_copy(h, 3).wait_recv()
+        flow = acc[h, 3] + yrecv[h, 3].astype(F32)
+        for j in range(3):
+            z_arrival(h, j).wait_recv()
+            flow = flow + zrecv[h, j].astype(F32)
+        flow_t[h] = flow
+        limit = pred_t[2]
+        grad = ((flow - pred_t[h]) + jax.nn.sigmoid(4.0 * (flow - limit))
+                - jax.nn.sigmoid(4.0 * (-flow - limit)))
+        ag[h, 3] = grad.astype(BF16)
+        for i in range(3):
+            az_copy(h, i).start()
+        ay_copy(h, 3).start()
+        ac_copy(h, 3).start()
+
+    def pass_z(h):
+        for i in range(3):
+            az_arrival(h, i).wait_recv()
+            ay_copy(h, i).start()
+            ac_copy(h, i).start()
+
+    def pass_y(h):
+        for i in (3, 0, 1, 2):
+            ay_copy(h, i).wait_recv()
+            ac_copy(h, 4 + i).start()
+
+    def backward(h, slot):
         zz = (z + 1 + slot % 4) % 4
         yy = (y + slot // 4) % 2
         cc = (c + slot // 8) % 2
         o = zz * 4 + yy * 2 + cc
-        return (jnp.dot(dense_t[o, 0], ag[slot], preferred_element_type=F32)
-                + jnp.dot(dense_t[o, 1], ag[slot], preferred_element_type=F32))
-
-    total = gx_own
-    total[...] = backward(3)
-
-    for i in range(3):
-        az_arrival(i).wait_recv()
-        ay_copy(i).start()
-        ac_copy(i).start()
-        total[...] += backward(i)
-    for i in (3, 0, 1, 2):
-        ay_copy(i).wait_recv()
-        ac_copy(4 + i).start()
-        total[...] += backward(4 + i)
-    for i in (3, 0, 1, 2, 7, 4, 5, 6):
-        ac_copy(i).wait_recv()
-        total[...] += backward(8 + i)
-
-    whole = total[...]
-    gx_send[...] = jnp.where(first, whole[:, 128:], whole[:, :128])
-    gx_copy = copy(gx_send, gx_recv, gx_sem.at[0], gx_sem.at[1], x_mate)
+        return (jnp.dot(dense_t[o, 0], ag[h, slot], preferred_element_type=F32)
+                + jnp.dot(dense_t[o, 1], ag[h, slot], preferred_element_type=F32))
+
+    def add_own(h):
+        def step(k, carry):
+            total[h] += backward(h, k)
+            return carry
+        total[h] = jnp.zeros((256, 128), F32)
+        lax.fori_loop(0, 8, step, 0)
+
+    def add_core(h):
+        for i in (3, 0, 1, 2, 7, 4, 5, 6):
+            ac_copy(h, i).wait_recv()
+            total[h] += backward(h, 8 + i)
+
+    finish(0)
+    fx_copy = copy(flow_t.at[0], fx_recv, fx_sem.at[0], fx_sem.at[1], x_mate)
+    fx_copy.start()
+    finish(1)
+    pass_z(0)
+    pass_y(0)
+    pass_z(1)
+    add_own(0)
+    add_core(0)
+    gx_copy = copy(total.at[0], gx_recv, gx_sem.at[0], gx_sem.at[1], x_mate)
     gx_copy.start()
-
-    fx_copy.wait_recv()
-    for m in range(3):
-        rows_m = pl.ds(m * 64, 64)
-        mine_m, other_m = fx_own[rows_m, :], fx_recv[rows_m, :]
-        top = jnp.where(first, mine_m, other_m)
-        low = jnp.where(first, other_m, mine_m)
-        fout_ref[:, pl.ds(m * 128, 128)] = jnp.concatenate([top, low], axis=0).T
-
-    kept = jnp.where(first, whole[:, :128], whole[:, 128:])
+    pass_y(1)
+    add_own(1)
+    add_core(1)
     gx_copy.wait_recv()
-    gsend[...] = (kept + gx_recv[...]).T.reshape(16, 8, 256).astype(BF16)
+    gsend[...] = (total[1] + gx_recv[...]).T.reshape(16, 8, 256).astype(BF16)
 
     def out_copy(k):
         d = (b + k) % 16
@@ -270,28 +297,37 @@
     lax.fori_loop(1, 16, out_start, 0)
     grecv[b] = gsend[b]
 
+    fx_copy.wait_recv()
+    for m in range(3):
+        rows_m = pl.ds(m * 64, 64)
+        mine_m, other_m = flow_t[1, rows_m, :], fx_recv[rows_m, :]
+        top = jnp.where(first, mine_m, other_m)
+        low = jnp.where(first, other_m, mine_m)
+        fout_ref[:, pl.ds(m * 128, 128)] = jnp.concatenate([top, low], axis=0).T
+
     def sent_inj(k, carry):
         inj_copy(k)[0].wait_send()
         return carry
 
     lax.fori_loop(1, 32, sent_inj, 0)
 
-    def sent_c(k, carry):
-        c_copy(k).wait_send()
-        ac_copy(k).wait_send()
-        return carry
-
-    lax.fori_loop(0, 8, sent_c, 0)
-
-    def sent_y(k, carry):
-        y_copy(k).wait_send()
-        ay_copy(k).wait_send()
-        return carry
-
-    lax.fori_loop(0, 4, sent_y, 0)
-    for i in range(3):
-        z_copy(i).wait_send()
-        az_copy(i).wait_send()
+    for h in range(2):
+        def sent_c(k, carry):
+            c_copy(h, k).wait_send()
+            ac_copy(h, k).wait_send()
+            return carry
+
+        lax.fori_loop(0, 8, sent_c, 0)
+
+        def sent_y(k, carry):
+            y_copy(h, k).wait_send()
+            ay_copy(h, k).wait_send()
+            return carry
+
+        lax.fori_loop(0, 4, sent_y, 0)
+        for i in range(3):
+            z_copy(h, i).wait_send()
+            az_copy(h, i).wait_send()
     pred_copy.wait_send()
     fx_copy.wait_send()
     gx_copy.wait_send()
@@ -314,44 +350,49 @@
 def fused(injections, tile_values, tile_line, tile_bus, flow_pred, line_limit):
     vmem = pl.BlockSpec(memory_space=pltpu.VMEM)
     dma = pltpu.SemaphoreType.DMA
-    block = (192, 256)
+    block, half = (192, 256), (192, 128)
     return pl.pallas_call(
         kernel,
         out_shape=(jax.ShapeDtypeStruct((8, 4096), BF16), jax.ShapeDtypeStruct((128, 384), F32)),
-        in_specs=[vmem] * 6,
+        in_specs=[pl.BlockSpec(memory_space=pl.ANY)] * 6,
         out_specs=(vmem, vmem),
         scratch_shapes=[
+            pltpu.VMEM((8, 4096), BF16),
+            pltpu.VMEM((64, 64, 128), BF16),
+            pltpu.VMEM((1, 64), jnp.int32),
+            pltpu.VMEM((1, 64), jnp.int32),
+            pltpu.VMEM((128, 384), BF16),
+            pltpu.VMEM((1, 384), jnp.int32),
             pltpu.VMEM((8, 128), jnp.int32),
             pltpu.SMEM((8, 128), jnp.int32),
             pltpu.VMEM((32, 8, 256), BF16),
             pltpu.VMEM((256, 256), BF16),
             pltpu.VMEM((16, 2) + block, BF16),
             pltpu.VMEM((16, 2, 256, 192), BF16),
-            pltpu.VMEM((8,) + block, BF16),
-            pltpu.VMEM((8,) + block, BF16),
-            pltpu.VMEM((4,) + block, BF16),
-            pltpu.VMEM((4,) + block, BF16),
-            pltpu.VMEM((4,) + block, F32),
-            pltpu.VMEM((3,) + block, BF16),
-            pltpu.VMEM((3,) + block, BF16),
+            pltpu.VMEM((2, 8) + half, BF16),
+            pltpu.VMEM((2, 8) + half, BF16),
+            pltpu.VMEM((2, 4) + half, BF16),
+            pltpu.VMEM((2, 4) + half, BF16),
+            pltpu.VMEM((4,) + half, F32),
+            pltpu.VMEM((2, 4) + half, F32),
+            pltpu.VMEM((2, 3) + half, BF16),
+            pltpu.VMEM((2, 3) + half, BF16),
             pltpu.VMEM((128, 384), BF16),
-            pltpu.VMEM((2,) + block, F32),
-            pltpu.VMEM((192, 128), F32),
-            pltpu.VMEM((192, 128), F32),
-            pltpu.VMEM((192, 128), F32),
-            pltpu.VMEM((16,) + block, BF16),
-            pltpu.VMEM((256, 128), F32),
-            pltpu.VMEM((256, 256), F32),
+            pltpu.VMEM((3,) + half, F32),
+            pltpu.VMEM((2,) + half, F32),
+            pltpu.VMEM(half, F32),
+            pltpu.VMEM((2, 16) + half, BF16),
+            pltpu.VMEM((2, 256, 128), F32),
             pltpu.VMEM((256, 128), F32),
             pltpu.VMEM((16, 8, 256), BF16),
             pltpu.VMEM((16, 8, 256), BF16),
-            dma, dma((32,)), dma((32,)), dma((2,)),
-            dma((8,)), dma((8,)), dma((4,)), dma((4,)), dma((3,)), dma((3,)),
-            dma((2,)), dma((3,)), dma((3,)), dma((4,)), dma((4,)), dma((8,)), dma((8,)),
+            dma((6,)), dma, dma((32,)), dma((32,)), dma((2,)),
+            dma((2, 8)), dma((2, 8)), dma((2, 4)), dma((2, 4)), dma((2, 3)), dma((2, 3)),
+            dma((2,)), dma((2, 3)), dma((2, 3)), dma((2, 4)), dma((2, 4)), dma((2, 8)), dma((2, 8)),
             dma((2,)), dma((16,)), dma((16,)),
         ],
         compiler_params=pltpu.CompilerParams(
-            collective_id=0, has_side_effects=True, vmem_limit_bytes=48 * 1024 * 1024),
+            collective_id=0, has_side_effects=True, vmem_limit_bytes=56 * 1024 * 1024),
     )(injections, tile_values, tile_line.reshape(1, -1), tile_bus.reshape(1, -1), flow_pred,
       line_limit.reshape(1, -1))
 

time: 63.4 us -> 58.2 us (0.918)
  Pallas kernels: 56.9 us -> 53 us
  local copies, waits for them, and re-layouts: 5.61 us -> 4.33 us
    pallas_call x1, Pallas kernels: 56.9 us -> 53 us  [fused(): pl.pallas_call(kernel, out_shape=(jax.ShapeDtypeStruct((8, 4096), BF16),...]
    unnamed x14 -> x4, local copies, waits for them, and re-layouts: 5.61 us -> 3.76 us
where the time goes in v2:
time: 58.2 us; the launch traced here: 58 us
  Pallas kernels  53 us (91%)
  local copies, waits for them, and re-layouts  4.33 us (7%)
  between operations  0.65 us (1%)
    pallas_call x1, Pallas kernels, fused(): pl.pallas_call(kernel, out_shape=(jax.ShapeDtypeStruct((8, 4096), BF16),...  53 us
    unnamed x4, local copies, waits for them, and re-layouts  3.76 us

profile of v2, /device:TPU:0, one launch (start us, length us, event | category | flops | bytes accessed | tf_op | source)
XLA Modules:
  0.0 58.0 jit_solution(9811408201381700908)
XLA Ops:
  0.6 0.0 copy-start
  0.6 0.7 %copy-done = s32[384]{0:T(512)S(1)} copy-done((s32[384]{0:T(512)S(1)}, s32[384]{0:T(512)}, u32[]{:S(2)}) %copy-start) | copy-done | bytes 1560
  1.3 0.6 reshape.15.lim_hbm
  1.9 53.0 %shard_map.77 = (bf16[8,4096]{1,0:T(8,128)(2,1)}, f32[128,384]{1,0:T(8,128)}) custom-call(bf16[8,4096]{1,0:T(8,128)(2,1)} %inj_hbm.1, bf16[64,64,128]{2,1,0:T(8,128)(2,1)} %tiles_hbm.1, s32[1,64]{1,0:T(1,128)} %bitcast.2, s32[1,64]{1,0:T(1,128)} %bitcast.3, bf16[128,384]{1,0:T(8,128)(2,1)} %pred_hbm.1, s32[1,384]{1,0:T(1,128)} %reshape.15.lim_hbm), custom_call_target="tpu_custom_call" | custom-call | tf_op jit(solution)/shard_map/pallas_call | solution.py:354
  54.9 1.5 %copy.10 = bf16[8,4096]{1,0:T(8,128)(2,1)} copy(bf16[8,4096]{1,0:T(8,128)(2,1)} %get-tuple-element.4) | data formatting | bytes 131072
  56.4 1.6 %copy.11 = f32[128,384]{1,0:T(8,128)} copy(f32[128,384]{1,0:T(8,128)} %get-tuple-element.5) | data formatting | bytes 393216
Async XLA Ops:
  0.6 0.7 %copy-start = (s32[384]{0:T(512)S(1)}, s32[384]{0:T(512)}, u32[]{:S(2)}) copy-start(s32[384]{0:T(512)} %param.11) | copy-start | bytes 4612

commit v3 on v2

--- a/solution.py
+++ b/solution.py
@@ -98,21 +98,22 @@
     to_smem.wait()
     loads[2].wait()
 
-    def build(o, carry):
+    def build(r, carry):
+        zz = (z + 1 + r % 4) % 4
+        yy = (y + (r // 4) % 2) % 2
+        cc = (c + r // 8) % 2
+        o = zz * 4 + yy * 2 + cc
         tiles = []
         for j in range(6):
             v = table_s[0, o * 6 + j]
             tiles.append((tiles_ref[v // 8].astype(F32), (v // 2) % 4, v % 2))
         for m in range(3):
             for bb in range(2):
-                total = jnp.zeros((64, 128), F32)
+                part = jnp.zeros((64, 128), F32)
                 for tile, blk, bus in tiles:
                     w = jnp.where((blk == m + 1) & (bus == bb), 1.0, 0.0).astype(F32)
-                    total = total + tile * w
-                hi = total.astype(BF16)
-                lo = (total - hi.astype(F32)).astype(BF16)
-                dense[o, 0, pl.ds(m * 64, 64), pl.ds(bb * 128, 128)] = hi
-                dense[o, 1, pl.ds(m * 64, 64), pl.ds(bb * 128, 128)] = lo
+                    part = part + tile * w
+                dense[r, pl.ds(m * 64, 64), pl.ds(bb * 128, 128)] = part.astype(BF16)
         return carry
 
     lax.fori_loop(0, 16, build, 0)
@@ -125,15 +126,9 @@
     turned = inj_buf[...].astype(F32).reshape(256, 256).T.astype(BF16)
     inj_t[...] = jnp.where(first, jnp.concatenate([turned[:, 128:], turned[:, :128]], axis=1), turned)
 
-    def forward(o):
-        return (jnp.dot(dense[o, 0], inj_t[...], preferred_element_type=F32)
-                + jnp.dot(dense[o, 1], inj_t[...], preferred_element_type=F32))
-
-    def owner(k, core):
-        far = k // 4
-        zz = (z + 1 + k % 4) % 4
-        yy = jnp.where(far == 0, 1 - y, y)
-        return zz * 4 + yy * 2 + core
+    def forward(group):
+        rows = dense[pl.ds(group * 4, 4)].reshape(768, 256)
+        return jnp.dot(rows, inj_t[...], preferred_element_type=F32).reshape(4, 192, 256)
 
     def c_copy(h, k):
         return copy(csend.at[h, k], crecv.at[h, k], c_ss.at[h, k], c_rs.at[h, k], core_mate)
@@ -147,65 +142,54 @@
     def z_arrival(h, j):
         return copy(zsend.at[h, j], zrecv.at[h, j], z_ss.at[h, j], z_rs.at[h, j], zdev(j))
 
-    def send_core(k, carry):
-        part = forward(owner(k, 1 - c)).astype(BF16)
-        csend[0, k] = part[:, :128]
-        c_copy(0, k).start()
-        csend[1, k] = part[:, 128:]
-        c_copy(1, k).start()
-        return carry
-
-    def send_y(k, carry):
-        part = forward(owner(k, c))
-        stash[k] = part[:, 128:]
-        c_copy(0, k).wait_recv()
-        ysend[0, k] = (part[:, :128] + crecv[0, k].astype(F32)).astype(BF16)
-        y_copy(0, k).start()
-        return carry
-
-    def send_y_late(k, carry):
-        c_copy(1, k).wait_recv()
-        ysend[1, k] = (stash[k] + crecv[1, k].astype(F32)).astype(BF16)
-        y_copy(1, k).start()
-        return carry
-
-    def keep(k, carry):
-        part = forward(owner(k, c))
-        c_copy(0, k).wait_recv()
-        acc[0, k - 4] = part[:, :128] + crecv[0, k].astype(F32)
-        c_copy(1, k).wait_recv()
-        acc[1, k - 4] = part[:, 128:] + crecv[1, k].astype(F32)
-        return carry
-
-    def turn(o, carry):
-        dense_t[o, 0] = dense[o, 0].T
-        dense_t[o, 1] = dense[o, 1].T
-        return carry
-
-    def send_z(h):
-        for i in range(3):
-            y_copy(h, i).wait_recv()
-            zsend[h, i] = (acc[h, i] + yrecv[h, i].astype(F32)).astype(BF16)
-            z_copy(h, i).start()
-
-    lax.fori_loop(0, 4, send_core, 0)
-    lax.fori_loop(0, 4, send_y, 0)
-    lax.fori_loop(4, 8, send_core, 0)
-    lax.fori_loop(0, 4, send_y_late, 0)
-    lax.fori_loop(4, 8, keep, 0)
-    send_z(0)
+    def send_core(group):
+        part = forward(2 + group).astype(BF16)
+        for h in range(2):
+            for i in range(4):
+                csend[h, group * 4 + i] = part[i, :, h * 128:h * 128 + 128]
+                c_copy(h, group * 4 + i).start()
+
+    def turn(group):
+        dense_t[group] = dense[pl.ds(group * 4, 4)].reshape(768, 256).T
+
+    def send_z(h, i):
+        y_copy(h, i).wait_recv()
+        zsend[h, i] = (acc[h, i] + yrecv[h, i].astype(F32)).astype(BF16)
+        z_copy(h, i).start()
+
+    send_core(1)
+    far = forward(1)
+    for i in range(4):
+        stash[i] = far[i, :, 128:]
+        c_copy(0, 4 + i).wait_recv()
+        ysend[0, i] = (far[i, :, :128] + crecv[0, 4 + i].astype(F32)).astype(BF16)
+        y_copy(0, i).start()
+    send_core(0)
+    for i in range(4):
+        c_copy(1, 4 + i).wait_recv()
+        ysend[1, i] = (stash[i] + crecv[1, 4 + i].astype(F32)).astype(BF16)
+        y_copy(1, i).start()
+    near = forward(0)
+    for h in range(2):
+        for i in range(4):
+            c_copy(h, i).wait_recv()
+            acc[h, i] = near[i, :, h * 128:h * 128 + 128] + crecv[h, i].astype(F32)
+    for i in range(3):
+        send_z(0, i)
+        turn(i)
     loads[4].wait()
     loads[5].wait()
     pred_copy.wait_recv()
     mine = pred_ref[...].astype(F32).T
     theirs = pred_recv[...].astype(F32).T
-    lim_all = jnp.broadcast_to(lim_ref[...].astype(F32) * 0.01, (128, 384)).T
+    lim_all = jnp.broadcast_to(lim_ref[...].astype(F32)[None, :] * 0.01, (128, 384)).T
     for m in range(3):
         upper, lower = slice(m * 128, m * 128 + 64), slice(m * 128 + 64, m * 128 + 128)
         for n, array in enumerate((theirs, mine, lim_all)):
             pred_t[n, pl.ds(m * 64, 64), :] = jnp.where(first, array[upper], array[lower])
-    send_z(1)
-    lax.fori_loop(0, 16, turn, 0)
+    for i in range(3):
+        send_z(1, i)
+    turn(3)
 
     def az_copy(h, i):
         return copy(ag.at[h, 3], ag.at[h, 2 - i], az_ss.at[h, i], az_rs.at[h, 2 - i], zdev(i))
@@ -246,25 +230,20 @@
             ay_copy(h, i).wait_recv()
             ac_copy(h, 4 + i).start()
 
-    def backward(h, slot):
-        zz = (z + 1 + slot % 4) % 4
-        yy = (y + slot // 4) % 2
-        cc = (c + slot // 8) % 2
-        o = zz * 4 + yy * 2 + cc
-        return (jnp.dot(dense_t[o, 0], ag[h, slot], preferred_element_type=F32)
-                + jnp.dot(dense_t[o, 1], ag[h, slot], preferred_element_type=F32))
+    def backward(h, group):
+        g = ag[h, pl.ds(group * 4, 4)].reshape(768, 128)
+        return jnp.dot(dense_t[group], g, preferred_element_type=F32)
 
     def add_own(h):
-        def step(k, carry):
-            total[h] += backward(h, k)
-            return carry
-        total[h] = jnp.zeros((256, 128), F32)
-        lax.fori_loop(0, 8, step, 0)
+        total[h] = backward(h, 0) + backward(h, 1)
 
     def add_core(h):
-        for i in (3, 0, 1, 2, 7, 4, 5, 6):
+        for i in (3, 0, 1, 2):
             ac_copy(h, i).wait_recv()
-            total[h] += backward(h, 8 + i)
+        total[h] += backward(h, 2)
+        for i in (7, 4, 5, 6):
+            ac_copy(h, i).wait_recv()
+        total[h] += backward(h, 3)
 
     finish(0)
     fx_copy = copy(flow_t.at[0], fx_recv, fx_sem.at[0], fx_sem.at[1], x_mate)
@@ -347,13 +326,23 @@
     lax.fori_loop(1, 16, sent_out, 0)
 
 
+def store_both(grad_src, flow_src, grad_dst, flow_dst, sems):
+    copies = [pltpu.make_async_copy(grad_src, grad_dst, sems.at[0]),
+              pltpu.make_async_copy(flow_src, flow_dst, sems.at[1])]
+    for item in copies:
+        item.start()
+    for item in copies:
+        item.wait()
+
+
 def fused(injections, tile_values, tile_line, tile_bus, flow_pred, line_limit):
     vmem = pl.BlockSpec(memory_space=pltpu.VMEM)
     dma = pltpu.SemaphoreType.DMA
     block, half = (192, 256), (192, 128)
-    return pl.pallas_call(
+    shapes = (jax.ShapeDtypeStruct((8, 4096), BF16), jax.ShapeDtypeStruct((128, 384), F32))
+    results = pl.pallas_call(
         kernel,
-        out_shape=(jax.ShapeDtypeStruct((8, 4096), BF16), jax.ShapeDtypeStruct((128, 384), F32)),
+        out_shape=shapes,
         in_specs=[pl.BlockSpec(memory_space=pl.ANY)] * 6,
         out_specs=(vmem, vmem),
         scratch_shapes=[
@@ -362,13 +351,13 @@
             pltpu.VMEM((1, 64), jnp.int32),
             pltpu.VMEM((1, 64), jnp.int32),
             pltpu.VMEM((128, 384), BF16),
-            pltpu.VMEM((1, 384), jnp.int32),
+            pltpu.VMEM((384,), jnp.int32),
             pltpu.VMEM((8, 128), jnp.int32),
             pltpu.SMEM((8, 128), jnp.int32),
             pltpu.VMEM((32, 8, 256), BF16),
             pltpu.VMEM((256, 256), BF16),
-            pltpu.VMEM((16, 2) + block, BF16),
-            pltpu.VMEM((16, 2, 256, 192), BF16),
+            pltpu.VMEM((16,) + block, BF16),
+            pltpu.VMEM((4, 256, 768), BF16),
             pltpu.VMEM((2, 8) + half, BF16),
             pltpu.VMEM((2, 8) + half, BF16),
             pltpu.VMEM((2, 4) + half, BF16),
@@ -394,7 +383,13 @@
         compiler_params=pltpu.CompilerParams(
             collective_id=0, has_side_effects=True, vmem_limit_bytes=56 * 1024 * 1024),
     )(injections, tile_values, tile_line.reshape(1, -1), tile_bus.reshape(1, -1), flow_pred,
-      line_limit.reshape(1, -1))
+      line_limit)
+    anywhere = pl.BlockSpec(memory_space=pl.ANY)
+    return pl.pallas_call(
+        store_both, out_shape=shapes, in_specs=[anywhere] * 2, out_specs=(anywhere, anywhere),
+        scratch_shapes=[dma((2,))],
+        compiler_params=pltpu.CompilerParams(vmem_limit_bytes=56 * 1024 * 1024),
+    )(*results)
 
 
 def per_device(injections, tile_values, tile_line, tile_bus, flow_pred, line_limit):

time: 58.2 us -> 62.4 us (1.072)
  Pallas kernels: 53 us -> 61.7 us
  local copies, waits for them, and re-layouts: 4.33 us -> 0 us
    pallas_call x1 -> x2, Pallas kernels: 53 us -> 61.7 us  [the longest x1 52.6 us: fused(): pl.pallas_call(kernel, out_shape=shapes, in_specs=[pl.BlockSpec(memory_sp...]
    unnamed x4 -> x0, local copies, waits for them, and re-layouts: 3.76 us -> none
where the time goes in v3:
time: 62.4 us; the launch traced here: 62.3 us
  Pallas kernels  61.7 us (99%)
  between operations  0.64 us (1%)
    pallas_call x1, Pallas kernels, fused(): pl.pallas_call(kernel, out_shape=shapes, in_specs=[pl.BlockSpec(memory_sp...  52.6 us
    pallas_call x1, Pallas kernels, fused(): pl.pallas_call(store_both, out_shape=shapes, in_specs=[anywhere] * 2, out...  9.06 us

profile of v3, /device:TPU:0, one launch (start us, length us, event | category | flops | bytes accessed | tf_op | source)
XLA Modules:
  0.0 62.3 jit_solution(2474375348046559343)
XLA Ops:
  0.6 52.6 %shard_map.77 = (bf16[8,4096]{1,0:T(8,128)(2,1)}, f32[128,384]{1,0:T(8,128)}) custom-call(bf16[8,4096]{1,0:T(8,128)(2,1)} %inj_hbm.1, bf16[64,64,128]{2,1,0:T(8,128)(2,1)} %tiles_hbm.1, s32[1,64]{1,0:T(1,128)} %bitcast.2, s32[1,64]{1,0:T(1,128)} %bitcast.3, bf16[128,384]{1,0:T(8,128)(2,1)} %pred_hbm.1, s32[384]{0:T(512)} %lim_hbm.1), custom_call_target="tpu_custom_call" | custom-call | tf_op jit(solution)/shard_map/pallas_call | solution.py:343
  53.2 9.1 %shard_map.78 = (bf16[8,4096]{1,0:T(8,128)(2,1)}, f32[128,384]{1,0:T(8,128)}) custom-call(bf16[8,4096]{1,0:T(8,128)(2,1)} %get-tuple-element.4.grad_src, f32[128,384]{1,0:T(8,128)} %get-tuple-element.5.flow_src), custom_call_target="tpu_custom_call" | custom-call | tf_op jit(solution)/shard_map/pallas_call | solution.py:388

commit v4 on v3

--- a/solution.py
+++ b/solution.py
@@ -326,21 +326,12 @@
     lax.fori_loop(1, 16, sent_out, 0)
 
 
-def store_both(grad_src, flow_src, grad_dst, flow_dst, sems):
-    copies = [pltpu.make_async_copy(grad_src, grad_dst, sems.at[0]),
-              pltpu.make_async_copy(flow_src, flow_dst, sems.at[1])]
-    for item in copies:
-        item.start()
-    for item in copies:
-        item.wait()
-
-
 def fused(injections, tile_values, tile_line, tile_bus, flow_pred, line_limit):
     vmem = pl.BlockSpec(memory_space=pltpu.VMEM)
     dma = pltpu.SemaphoreType.DMA
     block, half = (192, 256), (192, 128)
     shapes = (jax.ShapeDtypeStruct((8, 4096), BF16), jax.ShapeDtypeStruct((128, 384), F32))
-    results = pl.pallas_call(
+    return pl.pallas_call(
         kernel,
         out_shape=shapes,
         in_specs=[pl.BlockSpec(memory_space=pl.ANY)] * 6,
@@ -384,12 +375,6 @@
             collective_id=0, has_side_effects=True, vmem_limit_bytes=56 * 1024 * 1024),
     )(injections, tile_values, tile_line.reshape(1, -1), tile_bus.reshape(1, -1), flow_pred,
       line_limit)
-    anywhere = pl.BlockSpec(memory_space=pl.ANY)
-    return pl.pallas_call(
-        store_both, out_shape=shapes, in_specs=[anywhere] * 2, out_specs=(anywhere, anywhere),
-        scratch_shapes=[dma((2,))],
-        compiler_params=pltpu.CompilerParams(vmem_limit_bytes=56 * 1024 * 1024),
-    )(*results)
 
 
 def per_device(injections, tile_values, tile_line, tile_bus, flow_pred, line_limit):

time: 62.4 us -> 56.5 us (0.905)
  Pallas kernels: 61.7 us -> 52.6 us
  local copies, waits for them, and re-layouts: 0 us -> 3.09 us
    pallas_call x1 -> x0, Pallas kernels: 9.06 us -> none  [fused(): pl.pallas_call(store_both, out_shape=shapes, in_specs=[anywhere] * 2, out...]
    unnamed x0 -> x2, local copies, waits for them, and re-layouts: none -> 3.09 us
where the time goes in v4:
time: 56.5 us; the launch traced here: 56.3 us
  Pallas kernels  52.6 us (93%)
  local copies, waits for them, and re-layouts  3.09 us (5%)
  between operations  0.64 us (1%)
    pallas_call x1, Pallas kernels, fused(): pl.pallas_call(kernel, out_shape=shapes, in_specs=[pl.BlockSpec(memory_sp...  52.6 us
    unnamed x2, local copies, waits for them, and re-layouts  3.09 us

profile of v4, /device:TPU:0, one launch (start us, length us, event | category | flops | bytes accessed | tf_op | source)
XLA Modules:
  0.0 56.3 jit_solution(5674038572175738748)
XLA Ops:
  0.6 52.6 %shard_map.77 = (bf16[8,4096]{1,0:T(8,128)(2,1)}, f32[128,384]{1,0:T(8,128)}) custom-call(bf16[8,4096]{1,0:T(8,128)(2,1)} %inj_hbm.1, bf16[64,64,128]{2,1,0:T(8,128)(2,1)} %tiles_hbm.1, s32[1,64]{1,0:T(1,128)} %bitcast.2, s32[1,64]{1,0:T(1,128)} %bitcast.3, bf16[128,384]{1,0:T(8,128)(2,1)} %pred_hbm.1, s32[384]{0:T(512)} %lim_hbm.1), custom_call_target="tpu_custom_call" | custom-call | tf_op jit(solution)/shard_map/pallas_call | solution.py:334
  53.2 1.5 %copy.10 = bf16[8,4096]{1,0:T(8,128)(2,1)} copy(bf16[8,4096]{1,0:T(8,128)(2,1)} %get-tuple-element.4) | data formatting | bytes 131072
  54.7 1.6 %copy.11 = f32[128,384]{1,0:T(8,128)} copy(f32[128,384]{1,0:T(8,128)} %get-tuple-element.5) | data formatting | bytes 393216
